TPU v7x, 32 devices: a whole 2x2x4 slice. The times are simulated.
32 devices in a mesh: grp: 2 (over x), aux: 8 (over z, y), bas: 2 (over core).
Axes of the slice: x: 2, y: 2, z: 4, core: 2. Of those that a mesh axis runs over, the one named last changes fastest.
Arguments:
- integrals: float32 [32, 16, 128, 1024], P(('grp', 'aux'), 'bas'), parts along dimension 0, may hold values from -0.1875 to 0.1875
- block_counts: int32 [32, 16], P(('grp', 'aux'), 'bas'), parts along dimension 0, may hold values from 1 to 8
- partner_blocks: int32 [32, 16, 8], P(('grp', 'aux'), 'bas'), parts along dimension 0, may hold values from 0 to 79, as said below
- occupied_coeff: float32 [20480, 512], P(('grp', 'bas')), parts along dimension 0, may hold values from -0.72 to 0.72
Outputs:
- exchange_matrix: float32 [4096, 2048], P(('grp', 'aux'), 'bas'), parts along dimension 0
There are 2 independent parts, one for each index of `grp`. A program takes and returns all parts, laid end to end along the dimension named above; each array names one. Nothing has to cross between parts.
Inputs may be any that keep to these rules, and one draw needn't show every extreme that they name: `partner_blocks`: the 8 entries of a task's list are distinct shell block numbers; only the first block_counts of them are significant.
All inputs are finite; a program needn't handle non-finite values.
Results may differ from a plain program's by a relative error of at most 0.0003.
Values sent between devices are 32-bit elements; how exact they have to be, the bound alone decides.
A program may use at most 128 MiB of HBM per device.

v0:
```python
import jax
import jax.numpy as jnp
from jax import lax
from jax.sharding import PartitionSpec as P


def task_half(tile_block, block_total, block_list, coeff_all):
    block_width = tile_block.shape[0]
    initial = jnp.zeros((block_width, coeff_all.shape[1]), jnp.float32)

    def add_block(block_index, running):
        tile_piece = lax.dynamic_slice_in_dim(tile_block, block_index * block_width, block_width, 1)
        first_row = block_list[block_index] * block_width
        coeff_rows = lax.dynamic_slice_in_dim(coeff_all, first_row, block_width, 0)
        return running + jnp.dot(
            tile_piece,
            coeff_rows,
            precision=lax.Precision.HIGHEST,
            preferred_element_type=jnp.float32,
        )

    return lax.fori_loop(0, block_total, add_block, initial)


def half_all(tile_blocks, block_totals, block_lists, coeff_all):

    def one_task(task_item):
        return task_half(task_item[0], task_item[1], task_item[2], coeff_all)

    return lax.map(one_task, (tile_blocks, block_totals, block_lists))


def shards(integrals, block_counts, partner_blocks, occupied_coeff):
    aux_local, shell_local, block_width, row_span = integrals.shape
    task_count = aux_local * shell_local
    occupied = occupied_coeff.shape[1]
    flat_tiles = integrals.reshape(task_count, block_width, row_span)
    flat_counts = block_counts.reshape(task_count)
    flat_lists = partner_blocks.reshape(task_count, partner_blocks.shape[2])
    coeff_all = lax.all_gather(occupied_coeff, "bas", axis=0, tiled=True)
    halves = half_all(flat_tiles, flat_counts, flat_lists, coeff_all)
    halves_mine = halves.reshape(aux_local, shell_local * block_width, occupied)
    halves_full = lax.all_gather(halves_mine, "bas", axis=1, tiled=True)
    return lax.psum_scatter(
        jnp.einsum(
            "pro,pco->rc",
            halves_full,
            halves_mine,
            precision=lax.Precision.HIGHEST,
            preferred_element_type=jnp.float32,
        ),
        "aux",
        scatter_dimension=0,
        tiled=True,
    )


def solution(mesh):
    placed = (
        P(("grp", "aux"), "bas", None, None),
        P(("grp", "aux"), "bas"),
        P(("grp", "aux"), "bas", None),
        P(("grp", "bas"), None),
    )
    return jax.shard_map(
        shards, mesh=mesh, in_specs=placed, out_specs=P(("grp", "aux"), "bas"), check_vma=False
    )
```

profile of v0, /device:TPU:1, one launch (start us, length us, event | category | flops | bytes accessed | tf_op | source)
XLA Modules:
  0.0 747.3 jit_solution(11214723051731785476)
XLA Ops:
  7.4 39.9 %all-gather.3.cloned.1.call-done = f32[10240,512]{1,0:T(8,128)} async-done(((f32[5120,512]{1,0:T(8,128)}), f32[10240,512]{1,0:T(8,128)}) %all-gather.3.cloned.1.call-update) | async-done | bytes 20971536 | tf_op jit(solution)/shard_map/all_gather | solution.py:40
  47.3 212.0 %while.21 = (s32[]{:T(128)}, f32[16,128,512]{2,1,0:T(8,128)}, s32[16]{0:T(128)S(1)}, f32[16,128,1024]{2,1,0:T(8,128)}, s32[16,8]{1,0:T(8,128)}, /*index=5*/f32[1...) while((s32[]{:T(128)}, f32[16,128,512]{2,1,0:T(8,128)}, ...), condition=%wide.region_3.4_spmd, body=%wide.region_0.3_spmd.sunk | while | flops 100728848 | bytes 2688108 | solution.py:30
  49.7 14.1 %while.22 = (s32[]{:T(128)}, f32[128,512]{1,0:T(8,128)S(1)}, s32[]{:T(128)}, f32[128,1024]{1,0:T(8,128)S(1)}, s32[8]{0:T(128)S(1)}, /*index=5*/f32[10240,512]{1,...) while((s32[]{:T(128)}, f32[128,512]{1,0:T(8,128)S(1)}, ...), condition=%wide.region_2.2_spmd, body=%wide.region_1.1_spmd.sunk | while | flops 100728848 | bytes 852239 | solution.py:22
  55.1 1.4 convolution_add_fusion.2
  67.0 14.1 %while.22 = (s32[]{:T(128)}, f32[128,512]{1,0:T(8,128)S(1)}, s32[]{:T(128)}, f32[128,1024]{1,0:T(8,128)S(1)}, s32[8]{0:T(128)S(1)}, /*index=5*/f32[10240,512]{1,...) while((s32[]{:T(128)}, f32[128,512]{1,0:T(8,128)S(1)}, ...), condition=%wide.region_2.2_spmd, body=%wide.region_1.1_spmd.sunk | while | flops 100728848 | bytes 852239 | solution.py:22
  72.3 1.4 convolution_add_fusion.2
  75.7 1.4 convolution_add_fusion.2
  84.2 7.3 while.22
  86.2 1.4 convolution_add_fusion.2
  94.8 10.7 %while.22 = (s32[]{:T(128)}, f32[128,512]{1,0:T(8,128)S(1)}, s32[]{:T(128)}, f32[128,1024]{1,0:T(8,128)S(1)}, s32[8]{0:T(128)S(1)}, /*index=5*/f32[10240,512]{1,...) while((s32[]{:T(128)}, f32[128,512]{1,0:T(8,128)S(1)}, ...), condition=%wide.region_2.2_spmd, body=%wide.region_1.1_spmd.sunk | while | flops 100728848 | bytes 852239 | solution.py:22
  100.1 1.4 convolution_add_fusion.2
  103.5 1.4 convolution_add_fusion.2
  108.6 4.0 while.22
  115.8 10.7 %while.22 = (s32[]{:T(128)}, f32[128,512]{1,0:T(8,128)S(1)}, s32[]{:T(128)}, f32[128,1024]{1,0:T(8,128)S(1)}, s32[8]{0:T(128)S(1)}, /*index=5*/f32[10240,512]{1,...) while((s32[]{:T(128)}, f32[128,512]{1,0:T(8,128)S(1)}, ...), condition=%wide.region_2.2_spmd, body=%wide.region_1.1_spmd.sunk | while | flops 100728848 | bytes 852239 | solution.py:22
  129.7 7.3 while.22
  135.0 1.4 convolution_add_fusion.2
  140.2 7.3 while.22
  150.7 10.7 %while.22 = (s32[]{:T(128)}, f32[128,512]{1,0:T(8,128)S(1)}, s32[]{:T(128)}, f32[128,1024]{1,0:T(8,128)S(1)}, s32[8]{0:T(128)S(1)}, /*index=5*/f32[10240,512]{1,...) while((s32[]{:T(128)}, f32[128,512]{1,0:T(8,128)S(1)}, ...), condition=%wide.region_2.2_spmd, body=%wide.region_1.1_spmd.sunk | while | flops 100728848 | bytes 852239 | solution.py:22
  156.1 1.4 convolution_add_fusion.2
  159.4 1.4 convolution_add_fusion.2
  164.6 14.1 %while.22 = (s32[]{:T(128)}, f32[128,512]{1,0:T(8,128)S(1)}, s32[]{:T(128)}, f32[128,1024]{1,0:T(8,128)S(1)}, s32[8]{0:T(128)S(1)}, /*index=5*/f32[10240,512]{1,...) while((s32[]{:T(128)}, f32[128,512]{1,0:T(8,128)S(1)}, ...), condition=%wide.region_2.2_spmd, body=%wide.region_1.1_spmd.sunk | while | flops 100728848 | bytes 852239 | solution.py:22
  166.6 1.4 convolution_add_fusion.2
  181.8 10.7 %while.22 = (s32[]{:T(128)}, f32[128,512]{1,0:T(8,128)S(1)}, s32[]{:T(128)}, f32[128,1024]{1,0:T(8,128)S(1)}, s32[8]{0:T(128)S(1)}, /*index=5*/f32[10240,512]{1,...) while((s32[]{:T(128)}, f32[128,512]{1,0:T(8,128)S(1)}, ...), condition=%wide.region_2.2_spmd, body=%wide.region_1.1_spmd.sunk | while | flops 100728848 | bytes 852239 | solution.py:22
  187.2 1.4 convolution_add_fusion.2
  195.7 10.7 %while.22 = (s32[]{:T(128)}, f32[128,512]{1,0:T(8,128)S(1)}, s32[]{:T(128)}, f32[128,1024]{1,0:T(8,128)S(1)}, s32[8]{0:T(128)S(1)}, /*index=5*/f32[10240,512]{1,...) while((s32[]{:T(128)}, f32[128,512]{1,0:T(8,128)S(1)}, ...), condition=%wide.region_2.2_spmd, body=%wide.region_1.1_spmd.sunk | while | flops 100728848 | bytes 852239 | solution.py:22
  209.6 4.0 while.22
  216.7 14.1 %while.22 = (s32[]{:T(128)}, f32[128,512]{1,0:T(8,128)S(1)}, s32[]{:T(128)}, f32[128,1024]{1,0:T(8,128)S(1)}, s32[8]{0:T(128)S(1)}, /*index=5*/f32[10240,512]{1,...) while((s32[]{:T(128)}, f32[128,512]{1,0:T(8,128)S(1)}, ...), condition=%wide.region_2.2_spmd, body=%wide.region_1.1_spmd.sunk | while | flops 100728848 | bytes 852239 | solution.py:22
  234.0 14.1 %while.22 = (s32[]{:T(128)}, f32[128,512]{1,0:T(8,128)S(1)}, s32[]{:T(128)}, f32[128,1024]{1,0:T(8,128)S(1)}, s32[8]{0:T(128)S(1)}, /*index=5*/f32[10240,512]{1,...) while((s32[]{:T(128)}, f32[128,512]{1,0:T(8,128)S(1)}, ...), condition=%wide.region_2.2_spmd, body=%wide.region_1.1_spmd.sunk | while | flops 100728848 | bytes 852239 | solution.py:22
  251.2 7.3 while.22
  259.4 299.1 %all-gather.5.cloned.1.call-done = f32[2,2048,512]{2,1,0:T(8,128)} async-done(((f32[2,1024,512]{2,1,0:T(8,128)}), f32[2,2048,512]{2,1,0:T(8,128)}) %all-gather.5.cloned.1.call-update) | async-done | bytes 8388624 | tf_op jit(solution)/shard_map/all_gather | solution.py:43
  558.6 31.8 %convolution_bitcast_fusion = f32[2048,1024]{1,0:T(8,128)} fusion(f32[2,2048,512]{2,1,0:T(8,128)} %all-gather.5.cloned.1.call-done, f32[2,1024,512]{2,1,0:T(8,128)} %bitcast.26), kind=kOutput, calls=%fused_computation.8 | convolution fusion | flops 25769803776 | bytes 20971520 | tf_op jit(solution)/shard_map/pro,pco->rc/dot_general | solution.py:45
  590.4 150.4 %reduce-scatter.2.cloned.1.call-done = f32[256,1024]{1,0:T(8,128)} async-done(((f32[2048,1024]{1,0:T(8,128)}), f32[256,1024]{1,0:T(8,128)}) %reduce-scatter.2.cloned.1.call-update) | async-done | bytes 1048592 | tf_op jit(solution)/shard_map/reduce_scatter | solution.py:44
  (169 shorter events, 127.0 us)
Async XLA Ops:
  6.5 0.8 copy-start
  6.5 40.7 %all-gather.3.cloned.1.call-start = ((), (), s32[]{:S(2)}) async-start(), calls=%async_computation.1 | async-start | bytes 31457280 | tf_op jit(solution)/shard_map/all_gather | solution.py:40
  7.3 551.3 %all-gather.5.cloned.1.call-start = ((), (), s32[]{:S(2)}) async-start(), calls=%async_computation.2 | async-start | bytes 12582912 | tf_op jit(solution)/shard_map/all_gather | solution.py:43
  259.4 481.4 %reduce-scatter.2.cloned.1.call-start = ((), (), s32[]{:S(2)}) async-start(), calls=%async_computation.3 | async-start | bytes 9437184 | tf_op jit(solution)/shard_map/reduce_scatter | solution.py:44
Sparse Core Ops, SparseCore 0:
  8.9 38.3 all-gather.2
  259.5 299.0 all-gather.4
  590.5 150.2 reduce-scatter.1
where the time goes:
time: 756 us; the launch traced here: 747 us
  waiting for transfers between devices  490 us (65%)
  matrix products  92.6 us (12%)
  local copies, waits for them, and re-layouts  80.3 us (11%)
  loops' own time  71 us (9%)
  between operations  13.1 us (2%)
    all_gather x1, waiting for transfers between devices, shards(): halves_full = lax.all_gather(halves_mine, 'bas', axis=1, tiled=True)  299 us
    reduce_scatter x1, waiting for transfers between devices, shards(): lax.psum_scatter(jnp.einsum('pro,pco->rc', halves_full, halves_mine, prec...  150 us
    another operation x16, loops' own time, task_half(): return lax.fori_loop(0, block_total, add_block, initial)  70.7 us
    dot_general x45, matrix products, add_block(): jnp.dot(tile_piece, coeff_rows, precision=lax.Precision.HIGHEST, preferre...  60.8 us
    all_gather x1, waiting for transfers between devices, shards(): coeff_all = lax.all_gather(occupied_coeff, 'bas', axis=0, tiled=True)  39.9 us
    dot_general x1, matrix products, shards(): jnp.einsum('pro,pco->rc', halves_full, halves_mine, precision=lax.Precisi...  31.8 us
    dynamic_slice x45, local copies, waits for them, and re-layouts, add_block(): first_row = block_list[block_index] * block_width  29.8 us
    squeeze x32, local copies, waits for them, and re-layouts, half_all(): return lax.map(one_task, (tile_blocks, block_totals, block_lists))  28.3 us
  transfers between devices with their start and end apart: 3, of which 3 were waited for; matrix products, arithmetic and copies ran while one was open for 0% of the time, Pallas kernels for 0%

commit v1 on v0

v1 whole, which is shorter than its diff:
```python
import functools

import jax
import jax.numpy as jnp
from jax import lax
from jax.experimental import pallas as pl
from jax.experimental.pallas import tpu as pltpu
from jax.sharding import PartitionSpec as P

MESH = pl.DeviceIdType.MESH
VMEM_LIMIT = 58 * 1024 * 1024
PIECES = 4


def split(values):
    high = values.astype(jnp.bfloat16)
    low = (values - high.astype(jnp.float32)).astype(jnp.bfloat16)
    return high, low


def swap_kernel(pieces, mine_ref, other_ref, send_sem, recv_sem):
    partner = 1 - lax.axis_index("bas")
    barrier = pltpu.get_barrier_semaphore()
    pl.semaphore_signal(barrier, inc=1, device_id={"bas": partner}, device_id_type=MESH)
    pl.semaphore_wait(barrier, 1)
    rows = mine_ref.shape[0] // pieces
    copies = []
    for piece in range(pieces):
        part = pl.ds(piece * rows, rows)
        copy = pltpu.make_async_remote_copy(
            src_ref=mine_ref.at[part],
            dst_ref=other_ref.at[part],
            send_sem=send_sem.at[piece],
            recv_sem=recv_sem.at[piece],
            device_id={"bas": partner},
            device_id_type=MESH,
        )
        copy.start()
        copies.append(copy)
    for copy in copies:
        copy.wait()


def swap(mine):
    return pl.pallas_call(
        functools.partial(swap_kernel, PIECES),
        out_shape=jax.ShapeDtypeStruct(mine.shape, mine.dtype),
        in_specs=[pl.BlockSpec(memory_space=pl.ANY)],
        out_specs=pl.BlockSpec(memory_space=pl.ANY),
        scratch_shapes=[
            pltpu.SemaphoreType.DMA((PIECES,)),
            pltpu.SemaphoreType.DMA((PIECES,)),
        ],
        compiler_params=pltpu.CompilerParams(collective_id=0, has_side_effects=True),
        name="swap_coeff",
    )(mine)


def half_kernel(
    lists_ref, counts_ref, core_ref, tile_ref, mine_ref, other_ref, half_ref, rows_ref, sem
):
    task = pl.program_id(0)
    tasks = pl.num_programs(0)
    listed = lists_ref.shape[1]
    width = tile_ref.shape[0]
    local_blocks = mine_ref.shape[0] // width

    def fetch(which):
        slot = lax.rem(which, 2)
        for index in range(listed):
            block = lists_ref[which, index]
            owner = (block >= local_blocks).astype(jnp.int32)
            first = pl.multiple_of((block - owner * local_blocks) * width, width)
            place = rows_ref.at[slot, pl.ds(index * width, width)]

            @pl.when(owner == core_ref[0])
            def _():
                pltpu.make_async_copy(
                    mine_ref.at[pl.ds(first, width)], place, sem.at[slot]
                ).start()

            @pl.when(owner != core_ref[0])
            def _():
                pltpu.make_async_copy(
                    other_ref.at[pl.ds(first, width)], place, sem.at[slot]
                ).start()

    @pl.when(task == 0)
    def _():
        fetch(task)

    @pl.when(task + 1 < tasks)
    def _():
        fetch(task + 1)

    slot = lax.rem(task, 2)
    pltpu.make_async_copy(rows_ref.at[slot], rows_ref.at[slot], sem.at[slot]).wait()
    column = lax.broadcasted_iota(jnp.int32, tile_ref.shape, 1)
    tile = jnp.where(column < counts_ref[task] * width, tile_ref[...], 0.0)
    tile_high, tile_low = split(tile)
    row_high, row_low = split(rows_ref[slot])
    both = jnp.dot(
        jnp.concatenate([tile_high, tile_low], axis=0),
        row_high,
        preferred_element_type=jnp.float32,
    )
    cross = jnp.dot(tile_high, row_low, preferred_element_type=jnp.float32)
    half_ref[...] = both[:width] + (both[width:] + cross)


def half_all(tiles, counts, lists, mine, other):
    aux_local, shell_local, width, span = tiles.shape
    tasks = aux_local * shell_local
    occupied = mine.shape[1]
    core = lax.axis_index("bas").astype(jnp.int32).reshape(1)
    return pl.pallas_call(
        half_kernel,
        out_shape=jax.ShapeDtypeStruct((shell_local * width, aux_local * occupied), jnp.float32),
        grid_spec=pltpu.PrefetchScalarGridSpec(
            num_scalar_prefetch=3,
            grid=(tasks,),
            in_specs=[
                pl.BlockSpec((width, span), lambda task, *_: (task, 0)),
                pl.BlockSpec(memory_space=pl.ANY),
                pl.BlockSpec(memory_space=pl.ANY),
            ],
            out_specs=pl.BlockSpec(
                (width, occupied), lambda task, *_: (task % shell_local, task // shell_local)
            ),
            scratch_shapes=[
                pltpu.VMEM((2, span, occupied), jnp.float32),
                pltpu.SemaphoreType.DMA((2,)),
            ],
        ),
        compiler_params=pltpu.CompilerParams(vmem_limit_bytes=VMEM_LIMIT),
        name="half_transform",
    )(
        lists.reshape(tasks, lists.shape[2]),
        counts.reshape(tasks),
        core,
        tiles.reshape(tasks * width, span),
        mine,
        other,
    )


def exchange_kernel(
    aux,
    mine_ref,
    out_ref,
    other_ref,
    parts_ref,
    near_send,
    near_recv,
    sums_ref,
    far_recv,
    turn_send,
    turn_recv,
    half_sems,
    near_sems,
    far_sems,
    turn_sems,
):
    near_count = 2
    far_count = aux // near_count
    ring = aux // 2
    keep = ring // 2
    block = out_ref.shape[0]
    half_rows = mine_ref.shape[0]

    position = lax.axis_index("aux")
    core = lax.axis_index("bas")
    far = position // near_count
    near = lax.rem(position, near_count)

    barrier = pltpu.get_barrier_semaphore()
    me = position * 2 + core
    for step in range(1, 2 * aux):
        there = lax.rem(me + step, 2 * aux)
        pl.semaphore_signal(
            barrier,
            inc=1,
            device_id={"aux": there // 2, "bas": lax.rem(there, 2)},
            device_id_type=MESH,
        )
    pl.semaphore_wait(barrier, 2 * aux - 1)

    def remote(source, target, sems, index, device):
        return pltpu.make_async_remote_copy(
            src_ref=source,
            dst_ref=target,
            send_sem=sems.at[(0,) + index],
            recv_sem=sems.at[(1,) + index],
            device_id=device,
            device_id_type=MESH,
        )

    def half_copy(index):
        part = pl.ds(index * block, block)
        return remote(
            mine_ref.at[part], other_ref.at[part], half_sems, (index,), {"bas": 1 - core}
        )

    def near_copy(step, k):
        return remote(
            near_send.at[step, k],
            near_recv.at[step, k],
            near_sems,
            (step, k),
            {"aux": far * near_count + (1 - near)},
        )

    def far_copy(step, k):
        target = lax.rem(far + step + 1, far_count)
        return remote(
            sums_ref.at[step, k],
            far_recv.at[step, k],
            far_sems,
            (step, k),
            {"aux": target * near_count + near},
        )

    def in_half(far_index):
        return far_index // (far_count // 2) == core

    def column_of(row, k):
        local = lax.rem(row, ring)
        inside = (row // ring == core).astype(jnp.int32)
        return lax.rem(
            inside * (local + k) + (1 - inside) * (local - k - core + 2 * ring), ring
        )

    def turn_copy(k):
        inside = in_half(far).astype(jnp.int32)
        return remote(
            turn_send.at[k],
            turn_recv.at[k],
            turn_sems,
            (k,),
            {
                "aux": core * ring + column_of(position, k),
                "bas": inside * core + (1 - inside) * (1 - core),
            },
        )

    def blocks(far_index, work):
        for k in range(keep):
            work(k)
        pl.when(in_half(far_index))(functools.partial(work, keep))

    def store_parts(source, first, index):
        part = pl.ds(pl.multiple_of(index * block, block), block)
        high, low = split(source[part, :])
        start = pl.multiple_of((first + index) * 2 * block, 2 * block)
        parts_ref[pl.ds(start, block), :] = high
        parts_ref[pl.ds(start + block, block), :] = low

    def product(row, k):
        column = core * ring + column_of(row, k)
        row_at = pl.multiple_of(row * 2 * block, 2 * block)
        column_at = pl.multiple_of(column * 2 * block, 2 * block)
        contract = (((1,), (1,)), ((), ()))
        both = lax.dot_general(
            parts_ref[pl.ds(row_at, 2 * block), :],
            parts_ref[pl.ds(column_at, block), :],
            contract,
            preferred_element_type=jnp.float32,
        )
        cross = lax.dot_general(
            parts_ref[pl.ds(row_at, block), :],
            parts_ref[pl.ds(column_at + block, block), :],
            contract,
            preferred_element_type=jnp.float32,
        )
        return both[:block] + (both[block:] + cross)

    half_blocks = half_rows // block
    for index in range(half_blocks):
        half_copy(index).start()

    def split_mine(index, carry):
        store_parts(mine_ref, core * ring, index)
        return carry

    lax.fori_loop(0, half_blocks, split_mine, 0)

    def split_other(index, carry):
        half_copy(index).wait_recv()
        store_parts(other_ref, (1 - core) * ring, index)
        return carry

    lax.fori_loop(0, half_blocks, split_other, 0)

    def send_near(step, carry):
        target = lax.rem(far + step + 1, far_count)
        row = target * near_count + (1 - near)

        def work(k):
            near_send[step, k] = product(row, k)
            near_copy(step, k).start()

        blocks(target, work)
        return carry

    lax.fori_loop(0, far_count, send_near, 0)

    def own_products(step, carry):
        target = lax.rem(far + step + 1, far_count)

        def work(k):
            sums_ref[step, k] = product(target * near_count + near, k)

        blocks(target, work)
        return carry

    lax.fori_loop(0, far_count, own_products, 0)

    def send_far(step, carry):
        def work(k):
            near_copy(step, k).wait_recv()
            sums_ref[step, k] += near_recv[step, k]
            far_copy(step, k).start()

        blocks(lax.rem(far + step + 1, far_count), work)
        return carry

    lax.fori_loop(0, far_count - 1, send_far, 0)

    def finish(k):
        last = far_count - 1
        near_copy(last, k).wait_recv()
        total = sums_ref[last, k] + near_recv[last, k]
        for step in range(far_count - 1):
            far_copy(step, k).wait_recv()
            total += far_recv[step, k]
        at = pl.multiple_of(column_of(position, k) * block, block)
        out_ref[:, pl.ds(at, block)] = total
        return total

    def turned(k):
        turn_send[k] = finish(k).T
        turn_copy(k).start()

    def place(k):
        turn_copy(k).wait_recv()
        local = lax.rem(position, ring)
        inside = in_half(far).astype(jnp.int32)
        column = lax.rem(
            inside * (local - k + ring) + (1 - inside) * (local + k + 1 - core), ring
        )
        out_ref[:, pl.ds(pl.multiple_of(column * block, block), block)] = turn_recv[k]
        turn_copy(k).wait_send()

    here = in_half(far)
    there = jnp.logical_not(here)
    for k in range(1, keep):
        turned(k)

    @pl.when(here)
    def _():
        finish(0)
        finish(keep)

    pl.when(there)(functools.partial(turned, 0))
    for k in range(1, keep):
        place(k)
    pl.when(there)(functools.partial(place, 0))

    for index in range(half_blocks):
        half_copy(index).wait_send()

    def near_done(step, carry):
        blocks(
            lax.rem(far + step + 1, far_count), lambda k: near_copy(step, k).wait_send()
        )
        return carry

    lax.fori_loop(0, far_count, near_done, 0)

    def far_done(step, carry):
        blocks(
            lax.rem(far + step + 1, far_count), lambda k: far_copy(step, k).wait_send()
        )
        return carry

    lax.fori_loop(0, far_count - 1, far_done, 0)


def exchange(half, aux):
    half_rows, depth = half.shape
    block = 2 * half_rows // aux
    far_count = aux // 2
    slots = aux // 4 + 1
    square = (block, block)
    return pl.pallas_call(
        functools.partial(exchange_kernel, aux),
        out_shape=jax.ShapeDtypeStruct((block, half_rows), jnp.float32),
        in_specs=[pl.BlockSpec(memory_space=pltpu.VMEM)],
        out_specs=pl.BlockSpec(memory_space=pltpu.VMEM),
        scratch_shapes=[
            pltpu.VMEM((half_rows, depth), jnp.float32),
            pltpu.VMEM((4 * half_rows, depth), jnp.bfloat16),
            pltpu.VMEM((far_count, slots) + square, jnp.float32),
            pltpu.VMEM((far_count, slots) + square, jnp.float32),
            pltpu.VMEM((far_count, slots) + square, jnp.float32),
            pltpu.VMEM((far_count - 1, slots) + square, jnp.float32),
            pltpu.VMEM((slots,) + square, jnp.float32),
            pltpu.VMEM((slots,) + square, jnp.float32),
            pltpu.SemaphoreType.DMA((2, half_rows // block)),
            pltpu.SemaphoreType.DMA((2, far_count, slots)),
            pltpu.SemaphoreType.DMA((2, far_count - 1, slots)),
            pltpu.SemaphoreType.DMA((2, slots)),
        ],
        compiler_params=pltpu.CompilerParams(
            collective_id=1, has_side_effects=True, vmem_limit_bytes=VMEM_LIMIT
        ),
        name="exchange",
    )(half)


def shards(aux, integrals, block_counts, partner_blocks, occupied_coeff):
    other = swap(occupied_coeff)
    half = half_all(integrals, block_counts, partner_blocks, occupied_coeff, other)
    return exchange(half, aux)


def solution(mesh):
    placed = (
        P(("grp", "aux"), "bas", None, None),
        P(("grp", "aux"), "bas"),
        P(("grp", "aux"), "bas", None),
        P(("grp", "bas"), None),
    )
    return jax.shard_map(
        functools.partial(shards, mesh.shape["aux"]),
        mesh=mesh,
        in_specs=placed,
        out_specs=P(("grp", "aux"), "bas"),
        check_vma=False,
    )
```

time: 756 us -> 144 us (0.19); the launches traced: 747 us -> 144 us
  waiting for transfers between devices: 490 us -> 0 us
  Pallas kernels: 0 us -> 140 us
  matrix products: 92.6 us -> 0 us
  local copies, waits for them, and re-layouts: 80.3 us -> 3.58 us
  loops' own time: 71 us -> 0 us
  between operations: 13.1 us -> 0.03 us
    all_gather x2 -> x0, waiting for transfers between devices: 339 us -> none  [the longest x1 299 us: shards(): halves_full = lax.all_gather(halves_mine, 'bas', axis=1, tiled=True)]
    reduce_scatter x1 -> x0, waiting for transfers between devices: 150 us -> none  [shards(): lax.psum_scatter(jnp.einsum('pro,pco->rc', halves_full, halves_mine, prec...]
    pallas_call x0 -> x3, Pallas kernels: none -> 140 us  [the longest x1 100 us: exchange(): pl.pallas_call(functools.partial(exchange_kernel, aux), out_shape=jax.Sha...]
    dot_general x46 -> x0, matrix products: 92.6 us -> none  [the longest x45 60.8 us: add_block(): jnp.dot(tile_piece, coeff_rows, precision=lax.Precision.HIGHEST, preferre...]
    another operation x17 -> x0, loops' own time: 71 us -> none  [the longest x16 70.7 us: task_half(): return lax.fori_loop(0, block_total, add_block, initial)]
    dynamic_slice x61 -> x0, local copies, waits for them, and re-layouts: 40.1 us -> none  [the longest x45 29.8 us: add_block(): first_row = block_list[block_index] * block_width]
    squeeze x32 -> x0, local copies, waits for them, and re-layouts: 28.3 us -> none  [half_all(): return lax.map(one_task, (tile_blocks, block_totals, block_lists))]
    dynamic_update_slice x16 -> x0, local copies, waits for them, and re-layouts: 11.6 us -> none  [half_all(): return lax.map(one_task, (tile_blocks, block_totals, block_lists))]
  transfers between devices with their start and end apart: 3 -> 0, of which waited for: 3 -> 0; matrix products, arithmetic and copies ran while one was open for 0% -> 0% of each run, Pallas kernels for 0% -> 0%
where the time goes in v1:
time: 144 us
  Pallas kernels  140 us (97%)
  local copies, waits for them, and re-layouts  3.58 us (2%)
    pallas_call x1, Pallas kernels, exchange(): pl.pallas_call(functools.partial(exchange_kernel, aux), out_shape=jax.Sha...  100 us
    pallas_call x1, Pallas kernels, half_all(): pl.pallas_call(half_kernel, out_shape=jax.ShapeDtypeStruct((shell_local *...  23.4 us
    pallas_call x1, Pallas kernels, swap(): pl.pallas_call(functools.partial(swap_kernel, PIECES), out_shape=jax.Shap...  16.6 us

profile of v1, /device:TPU:1, one launch (start us, length us, event | category | flops | bytes accessed | tf_op | source)
XLA Modules:
  0.0 143.5 jit_solution(9446854484881992100)
XLA Ops:
  0.0 1.3 reshape.13.counts_ref
  1.3 16.6 %swap_coeff.1.other_ref = f32[5120,512]{1,0:T(8,128)} custom-call(f32[5120,512]{1,0:T(8,128)} %mine_ref.3), custom_call_target="tpu_custom_call" | custom-call | tf_op jit(solution)/shard_map/swap_coeff/pallas_call | solution.py:45
  17.8 23.4 %half_transform.1.mine_ref = f32[1024,1024]{1,0:T(8,128)} custom-call(s32[16,8]{1,0:T(8,128)} %bitcast.4, s32[16]{0:T(128)} %reshape.13.counts_ref, s32[1]{0:T(128)} %bitcast.1.core_ref, f32[2048,1024]{1,0:T(8,128)} %bitcast.3, f32[5120,512]{1,0:T(8,128)} %mine_ref.3, f32[5120,512]{1,0:T(8,128)} %swap_coeff.1.other_ref), custom_call_target="tpu_custom_call" | custom-call | tf_op jit(solution)/shard_map/half_transform/pallas_call | solution.py:116
  41.2 100.0 %exchange.1 = f32[256,1024]{1,0:T(8,128)} custom-call(f32[1024,1024]{1,0:T(8,128)} %half_transform.1.mine_ref), custom_call_target="tpu_custom_call" | custom-call | tf_op jit(solution)/shard_map/exchange/pallas_call | solution.py:395
  141.2 2.3 %copy.9 = f32[256,1024]{1,0:T(8,128)} copy(f32[256,1024]{1,0:T(8,128)} %exchange.1) | data formatting | bytes 2097152

commit v2 on v1

--- a/solution.py
+++ b/solution.py
@@ -210,15 +210,37 @@
             {"aux": far * near_count + (1 - near)},
         )
 
-    def far_copy(step, k):
-        target = lax.rem(far + step + 1, far_count)
-        return remote(
-            sums_ref.at[step, k],
-            far_recv.at[step, k],
-            far_sems,
-            (step, k),
-            {"aux": target * near_count + near},
-        )
+    def far_copy(target, k):
+        down = (target < far).astype(jnp.int32)
+        last = down * (target == far - 1).astype(jnp.int32)
+        place = target + last * (far_count - target)
+        return pltpu.make_async_remote_copy(
+            src_ref=sums_ref.at[target, k],
+            dst_ref=far_recv.at[place, k],
+            send_sem=far_sems.at[0, target, k],
+            recv_sem=far_sems.at[1, place, k],
+            device_id={"aux": (far + 1 - 2 * down) * near_count + near},
+            device_id_type=MESH,
+        )
+
+    def add_far(place, k, target):
+        pltpu.make_async_copy(
+            far_recv.at[place, k], far_recv.at[place, k], far_sems.at[1, place, k]
+        ).wait()
+        sums_ref[target, k] += far_recv[place, k]
+
+    def target_at(step):
+        upper = (far >= far_count // 2).astype(jnp.int32)
+        low = far + upper * (far_count - 1 - 2 * far)
+        beyond = far_count - 1 - low
+        first = (step < beyond).astype(jnp.int32)
+        own = (step == far_count - 1).astype(jnp.int32)
+        target = (
+            first * (far_count - 1 - step)
+            + (1 - first) * (1 - own) * (step - beyond)
+            + own * low
+        )
+        return target + upper * (far_count - 1 - 2 * target)
 
     def in_half(far_index):
         return far_index // (far_count // 2) == core
@@ -292,12 +314,12 @@
     lax.fori_loop(0, half_blocks, split_other, 0)
 
     def send_near(step, carry):
-        target = lax.rem(far + step + 1, far_count)
+        target = target_at(step)
         row = target * near_count + (1 - near)
 
         def work(k):
-            near_send[step, k] = product(row, k)
-            near_copy(step, k).start()
+            near_send[target, k] = product(row, k)
+            near_copy(target, k).start()
 
         blocks(target, work)
         return carry
@@ -305,10 +327,10 @@
     lax.fori_loop(0, far_count, send_near, 0)
 
     def own_products(step, carry):
-        target = lax.rem(far + step + 1, far_count)
+        target = target_at(step)
 
         def work(k):
-            sums_ref[step, k] = product(target * near_count + near, k)
+            sums_ref[target, k] = product(target * near_count + near, k)
 
         blocks(target, work)
         return carry
@@ -316,23 +338,40 @@
     lax.fori_loop(0, far_count, own_products, 0)
 
     def send_far(step, carry):
+        target = target_at(step)
+        between = jnp.logical_or(
+            jnp.logical_and(target > far, far > 0),
+            jnp.logical_and(target < far, far < far_count - 1),
+        )
+
         def work(k):
-            near_copy(step, k).wait_recv()
-            sums_ref[step, k] += near_recv[step, k]
-            far_copy(step, k).start()
-
-        blocks(lax.rem(far + step + 1, far_count), work)
+            near_copy(target, k).wait_recv()
+            sums_ref[target, k] += near_recv[target, k]
+
+            @pl.when(between)
+            def _():
+                add_far(target, k, target)
+
+            far_copy(target, k).start()
+
+        blocks(target, work)
         return carry
 
     lax.fori_loop(0, far_count - 1, send_far, 0)
 
     def finish(k):
-        last = far_count - 1
-        near_copy(last, k).wait_recv()
-        total = sums_ref[last, k] + near_recv[last, k]
-        for step in range(far_count - 1):
-            far_copy(step, k).wait_recv()
-            total += far_recv[step, k]
+        near_copy(far, k).wait_recv()
+        sums_ref[far, k] += near_recv[far, k]
+
+        @pl.when(far > 0)
+        def _():
+            add_far(far, k, far)
+
+        @pl.when(far < far_count - 1)
+        def _():
+            add_far(far_count, k, far)
+
+        total = sums_ref[far, k]
         at = pl.multiple_of(column_of(position, k) * block, block)
         out_ref[:, pl.ds(at, block)] = total
         return total
@@ -370,17 +409,15 @@
         half_copy(index).wait_send()
 
     def near_done(step, carry):
-        blocks(
-            lax.rem(far + step + 1, far_count), lambda k: near_copy(step, k).wait_send()
-        )
+        target = target_at(step)
+        blocks(target, lambda k: near_copy(target, k).wait_send())
         return carry
 
     lax.fori_loop(0, far_count, near_done, 0)
 
     def far_done(step, carry):
-        blocks(
-            lax.rem(far + step + 1, far_count), lambda k: far_copy(step, k).wait_send()
-        )
+        target = target_at(step)
+        blocks(target, lambda k: far_copy(target, k).wait_send())
         return carry
 
     lax.fori_loop(0, far_count - 1, far_done, 0)
@@ -403,12 +440,12 @@
             pltpu.VMEM((far_count, slots) + square, jnp.float32),
             pltpu.VMEM((far_count, slots) + square, jnp.float32),
             pltpu.VMEM((far_count, slots) + square, jnp.float32),
-            pltpu.VMEM((far_count - 1, slots) + square, jnp.float32),
+            pltpu.VMEM((far_count + 1, slots) + square, jnp.float32),
             pltpu.VMEM((slots,) + square, jnp.float32),
             pltpu.VMEM((slots,) + square, jnp.float32),
             pltpu.SemaphoreType.DMA((2, half_rows // block)),
             pltpu.SemaphoreType.DMA((2, far_count, slots)),
-            pltpu.SemaphoreType.DMA((2, far_count - 1, slots)),
+            pltpu.SemaphoreType.DMA((2, far_count + 1, slots)),
             pltpu.SemaphoreType.DMA((2, slots)),
         ],
         compiler_params=pltpu.CompilerParams(

time: 144 us -> 135 us (0.938)
  Pallas kernels: 140 us -> 131 us
    pallas_call x1, Pallas kernels: 100 us -> 91.1 us  [exchange(): pl.pallas_call(functools.partial(exchange_kernel, aux), out_shape=jax.Sha...]
where the time goes in v2:
time: 135 us
  Pallas kernels  131 us (97%)
  local copies, waits for them, and re-layouts  3.58 us (3%)
    pallas_call x1, Pallas kernels, exchange(): pl.pallas_call(functools.partial(exchange_kernel, aux), out_shape=jax.Sha...  91.1 us
    pallas_call x1, Pallas kernels, half_all(): pl.pallas_call(half_kernel, out_shape=jax.ShapeDtypeStruct((shell_local *...  23.3 us
    pallas_call x1, Pallas kernels, swap(): pl.pallas_call(functools.partial(swap_kernel, PIECES), out_shape=jax.Shap...  16.6 us

profile of v2, /device:TPU:1, one launch (start us, length us, event | category | flops | bytes accessed | tf_op | source)
XLA Modules:
  0.0 134.6 jit_solution(8040026393592189165)
XLA Ops:
  0.0 1.3 reshape.13.counts_ref
  1.3 16.6 %swap_coeff.1.other_ref = f32[5120,512]{1,0:T(8,128)} custom-call(f32[5120,512]{1,0:T(8,128)} %mine_ref.3), custom_call_target="tpu_custom_call" | custom-call | tf_op jit(solution)/shard_map/swap_coeff/pallas_call | solution.py:45
  17.8 23.3 %half_transform.1.mine_ref = f32[1024,1024]{1,0:T(8,128)} custom-call(s32[16,8]{1,0:T(8,128)} %bitcast.4, s32[16]{0:T(128)} %reshape.13.counts_ref, s32[1]{0:T(128)} %bitcast.1.core_ref, f32[2048,1024]{1,0:T(8,128)} %bitcast.3, f32[5120,512]{1,0:T(8,128)} %mine_ref.3, f32[5120,512]{1,0:T(8,128)} %swap_coeff.1.other_ref), custom_call_target="tpu_custom_call" | custom-call | tf_op jit(solution)/shard_map/half_transform/pallas_call | solution.py:116
  41.2 91.1 %exchange.1 = f32[256,1024]{1,0:T(8,128)} custom-call(f32[1024,1024]{1,0:T(8,128)} %half_transform.1.mine_ref), custom_call_target="tpu_custom_call" | custom-call | tf_op jit(solution)/shard_map/exchange/pallas_call | solution.py:432
  132.3 2.3 %copy.9 = f32[256,1024]{1,0:T(8,128)} copy(f32[256,1024]{1,0:T(8,128)} %exchange.1) | data formatting | bytes 2097152

commit v3 on v2

v3 whole, which is shorter than its diff:
```python
import functools

import jax
import jax.numpy as jnp
from jax import lax
from jax.experimental import pallas as pl
from jax.experimental.pallas import tpu as pltpu
from jax.sharding import PartitionSpec as P

MESH = pl.DeviceIdType.MESH
VMEM_LIMIT = 58 * 1024 * 1024
PIECES = 10
SLOTS = 4


def split(values):
    high = values.astype(jnp.bfloat16)
    low = (values - high.astype(jnp.float32)).astype(jnp.bfloat16)
    return high, low


def exchange_kernel(
    aux,
    lists_ref,
    counts_ref,
    tiles_ref,
    coeff_ref,
    out_ref,
    land_ref,
    high_ref,
    low_ref,
    stage_ref,
    tile_ref,
    other_ref,
    parts_ref,
    near_recv,
    far_recv,
    turn_send,
    turn_recv,
    stage_sems,
    tile_sems,
    coeff_sems,
    half_sems,
    near_sems,
    far_sems,
    turn_sems,
):
    near_count = 2
    far_count = aux // near_count
    ring = aux // 2
    keep = ring // 2
    block = out_ref.shape[0]
    aux_local, shell_local, width, span = tiles_ref.shape
    tasks = aux_local * shell_local
    listed = lists_ref.shape[2]
    coeff_rows, occupied = coeff_ref.shape
    piece_rows = coeff_rows // PIECES
    slots = keep + 1
    across = occupied // block

    position = lax.axis_index("aux")
    core = lax.axis_index("bas")
    far = position // near_count
    near = lax.rem(position, near_count)

    def tile_copy(task):
        slot = lax.rem(task, SLOTS)
        return pltpu.make_async_copy(
            tiles_ref.at[task // shell_local, lax.rem(task, shell_local)],
            tile_ref.at[slot],
            tile_sems.at[slot],
        )

    def piece_at(piece):
        return pl.ds(pl.multiple_of(piece * piece_rows, piece_rows), piece_rows)

    def stage_copy(piece):
        slot = lax.rem(piece, 2)
        return pltpu.make_async_copy(
            coeff_ref.at[piece_at(piece)], stage_ref.at[slot], stage_sems.at[slot]
        )

    stage_copy(0).start()
    for task in range(SLOTS):
        tile_copy(task).start()

    barrier = pltpu.get_barrier_semaphore()
    me = position * 2 + core
    for step in range(1, 2 * aux):
        there = lax.rem(me + step, 2 * aux)
        pl.semaphore_signal(
            barrier,
            inc=1,
            device_id={"aux": there // 2, "bas": lax.rem(there, 2)},
            device_id_type=MESH,
        )
    pl.semaphore_wait(barrier, 2 * aux - 1)

    def remote(source, target, sems, index, device):
        return pltpu.make_async_remote_copy(
            src_ref=source,
            dst_ref=target,
            send_sem=sems.at[(0,) + index],
            recv_sem=sems.at[(1,) + index],
            device_id=device,
            device_id_type=MESH,
        )

    def coeff_copy(piece):
        part = piece_at(piece)
        return remote(
            coeff_ref.at[part], land_ref.at[part], coeff_sems, (piece,), {"bas": 1 - core}
        )

    def task_at(task):
        return pl.ds(pl.multiple_of(task * width, width), width)

    def half_copy(task):
        part = task_at(task)
        return remote(
            land_ref.at[part], other_ref.at[part], half_sems, (task,), {"bas": 1 - core}
        )

    def spare(number):
        row = tasks * width + (number // across) * block
        column = lax.rem(number, across) * block
        return (
            pl.ds(pl.multiple_of(row, block), block),
            pl.ds(pl.multiple_of(column, block), block),
        )

    def near_at(target, k):
        return spare(target * slots + k)

    def sum_at(target, k):
        return spare((far_count + target) * slots + k)

    def near_copy(step, k):
        return remote(
            land_ref.at[near_at(step, k)],
            near_recv.at[step, k],
            near_sems,
            (step, k),
            {"aux": far * near_count + (1 - near)},
        )

    def far_copy(target, k):
        down = (target < far).astype(jnp.int32)
        last = down * (target == far - 1).astype(jnp.int32)
        place = target + last * (far_count - target)
        return pltpu.make_async_remote_copy(
            src_ref=land_ref.at[sum_at(target, k)],
            dst_ref=far_recv.at[place, k],
            send_sem=far_sems.at[0, target, k],
            recv_sem=far_sems.at[1, place, k],
            device_id={"aux": (far + 1 - 2 * down) * near_count + near},
            device_id_type=MESH,
        )

    def add_far(place, k, target):
        pltpu.make_async_copy(
            far_recv.at[place, k], far_recv.at[place, k], far_sems.at[1, place, k]
        ).wait()
        land_ref[sum_at(target, k)] += far_recv[place, k]

    def target_at(step):
        upper = (far >= far_count // 2).astype(jnp.int32)
        low = far + upper * (far_count - 1 - 2 * far)
        beyond = far_count - 1 - low
        first = (step < beyond).astype(jnp.int32)
        own = (step == far_count - 1).astype(jnp.int32)
        target = (
            first * (far_count - 1 - step)
            + (1 - first) * (1 - own) * (step - beyond)
            + own * low
        )
        return target + upper * (far_count - 1 - 2 * target)

    def in_half(far_index):
        return far_index // (far_count // 2) == core

    def column_of(row, k):
        local = lax.rem(row, ring)
        inside = (row // ring == core).astype(jnp.int32)
        return lax.rem(
            inside * (local + k) + (1 - inside) * (local - k - core + 2 * ring), ring
        )

    def turn_copy(k):
        inside = in_half(far).astype(jnp.int32)
        return remote(
            turn_send.at[k],
            turn_recv.at[k],
            turn_sems,
            (k,),
            {
                "aux": core * ring + column_of(position, k),
                "bas": inside * core + (1 - inside) * (1 - core),
            },
        )

    def blocks(far_index, work):
        for k in range(keep):
            work(k)
        pl.when(in_half(far_index))(functools.partial(work, keep))

    def store_parts(values, half, task):
        row = half * (shell_local * width) + lax.rem(task, shell_local) * width
        start = (row // block) * 2 * block + lax.rem(row, block)
        columns = pl.ds(
            pl.multiple_of((task // shell_local) * occupied, occupied), occupied
        )
        high, low = split(values)
        parts_ref[pl.ds(pl.multiple_of(start, width), width), columns] = high
        parts_ref[pl.ds(pl.multiple_of(start + block, width), width), columns] = low

    def product(row, k):
        column = core * ring + column_of(row, k)
        row_at = pl.multiple_of(row * 2 * block, 2 * block)
        column_at = pl.multiple_of(column * 2 * block, 2 * block)
        contract = (((1,), (1,)), ((), ()))
        both = lax.dot_general(
            parts_ref[pl.ds(row_at, 2 * block), :],
            parts_ref[pl.ds(column_at, block), :],
            contract,
            preferred_element_type=jnp.float32,
        )
        cross = lax.dot_general(
            parts_ref[pl.ds(row_at, block), :],
            parts_ref[pl.ds(column_at + block, block), :],
            contract,
            preferred_element_type=jnp.float32,
        )
        return both[:block] + (both[block:] + cross)

    for piece in range(PIECES):
        coeff_copy(piece).start()

    def store_rows(values, half, piece):
        group = piece_rows // width
        first = half * (coeff_rows // width) + piece * group
        for index in range(group):
            part = values[index * width : (index + 1) * width]
            high_ref[first + index], low_ref[first + index] = split(part)

    def split_mine(piece, carry):
        pl.when(piece + 1 < PIECES)(lambda: stage_copy(piece + 1).start())
        stage_copy(piece).wait()
        store_rows(stage_ref[lax.rem(piece, 2)], core, piece)
        return carry

    lax.fori_loop(0, PIECES, split_mine, 0)

    def split_landed(piece, carry):
        coeff_copy(piece).wait_recv()
        store_rows(land_ref[piece_at(piece), :], 1 - core, piece)
        return carry

    lax.fori_loop(0, PIECES, split_landed, 0)

    def one_task(task, carry):
        tile_copy(task).wait()
        first, second = task // shell_local, lax.rem(task, shell_local)
        column = lax.broadcasted_iota(jnp.int32, (width, span), 1)
        tile = jnp.where(
            column < counts_ref[first, second] * width, tile_ref[lax.rem(task, SLOTS)], 0.0
        )
        blocks_here = [lists_ref[first, second, index] for index in range(listed)]
        row_high = jnp.concatenate([high_ref[block] for block in blocks_here], axis=0)
        row_low = jnp.concatenate([low_ref[block] for block in blocks_here], axis=0)
        tile_high, tile_low = split(tile)
        both = jnp.dot(
            jnp.concatenate([tile_high, tile_low], axis=0),
            row_high,
            preferred_element_type=jnp.float32,
        )
        cross = jnp.dot(tile_high, row_low, preferred_element_type=jnp.float32)
        half = both[:width] + (both[width:] + cross)
        land_ref[task_at(task), :] = half
        half_copy(task).start()
        store_parts(half, core, task)
        pl.when(task + SLOTS < tasks)(lambda: tile_copy(task + SLOTS).start())
        return carry

    lax.fori_loop(0, tasks, one_task, 0)

    def split_other(task, carry):
        half_copy(task).wait_recv()
        store_parts(other_ref[task_at(task), :], 1 - core, task)
        return carry

    lax.fori_loop(0, tasks, split_other, 0)

    def send_near(step, carry):
        target = target_at(step)
        row = target * near_count + (1 - near)

        def work(k):
            land_ref[near_at(target, k)] = product(row, k)
            near_copy(target, k).start()

        blocks(target, work)
        return carry

    lax.fori_loop(0, far_count, send_near, 0)

    def own_products(step, carry):
        target = target_at(step)

        def work(k):
            land_ref[sum_at(target, k)] = product(target * near_count + near, k)

        blocks(target, work)
        return carry

    lax.fori_loop(0, far_count, own_products, 0)

    def send_far(step, carry):
        target = target_at(step)
        between = jnp.logical_or(
            jnp.logical_and(target > far, far > 0),
            jnp.logical_and(target < far, far < far_count - 1),
        )

        def work(k):
            near_copy(target, k).wait_recv()
            land_ref[sum_at(target, k)] += near_recv[target, k]

            @pl.when(between)
            def _():
                add_far(target, k, target)

            far_copy(target, k).start()

        blocks(target, work)
        return carry

    lax.fori_loop(0, far_count - 1, send_far, 0)

    def finish(k):
        near_copy(far, k).wait_recv()
        land_ref[sum_at(far, k)] += near_recv[far, k]

        @pl.when(far > 0)
        def _():
            add_far(far, k, far)

        @pl.when(far < far_count - 1)
        def _():
            add_far(far_count, k, far)

        total = land_ref[sum_at(far, k)]
        at = pl.multiple_of(column_of(position, k) * block, block)
        out_ref[:, pl.ds(at, block)] = total
        return total

    def turned(k):
        turn_send[k] = finish(k).T
        turn_copy(k).start()

    def place(k):
        turn_copy(k).wait_recv()
        local = lax.rem(position, ring)
        inside = in_half(far).astype(jnp.int32)
        column = lax.rem(
            inside * (local - k + ring) + (1 - inside) * (local + k + 1 - core), ring
        )
        out_ref[:, pl.ds(pl.multiple_of(column * block, block), block)] = turn_recv[k]
        turn_copy(k).wait_send()

    here = in_half(far)
    there = jnp.logical_not(here)
    for k in range(1, keep):
        turned(k)

    @pl.when(here)
    def _():
        finish(0)
        finish(keep)

    pl.when(there)(functools.partial(turned, 0))
    for k in range(1, keep):
        place(k)
    pl.when(there)(functools.partial(place, 0))

    def coeff_done(piece, carry):
        coeff_copy(piece).wait_send()
        return carry

    lax.fori_loop(0, PIECES, coeff_done, 0)

    def half_done(task, carry):
        half_copy(task).wait_send()
        return carry

    lax.fori_loop(0, tasks, half_done, 0)

    def near_done(step, carry):
        target = target_at(step)
        blocks(target, lambda k: near_copy(target, k).wait_send())
        return carry

    lax.fori_loop(0, far_count, near_done, 0)

    def far_done(step, carry):
        target = target_at(step)
        blocks(target, lambda k: far_copy(target, k).wait_send())
        return carry

    lax.fori_loop(0, far_count - 1, far_done, 0)


def shards(aux, integrals, block_counts, partner_blocks, occupied_coeff):
    aux_local, shell_local, width, span = integrals.shape
    coeff_rows, occupied = occupied_coeff.shape
    tasks = aux_local * shell_local
    half_rows = shell_local * width
    block = 2 * half_rows // aux
    far_count = aux // 2
    slots = aux // 4 + 1
    square = (block, block)
    spares = -(-2 * far_count * slots // (occupied // block)) * block
    return pl.pallas_call(
        functools.partial(exchange_kernel, aux),
        out_shape=jax.ShapeDtypeStruct((block, half_rows), jnp.float32),
        in_specs=[
            pl.BlockSpec(memory_space=pltpu.SMEM),
            pl.BlockSpec(memory_space=pltpu.SMEM),
            pl.BlockSpec(memory_space=pl.ANY),
            pl.BlockSpec(memory_space=pl.ANY),
        ],
        out_specs=pl.BlockSpec(memory_space=pltpu.VMEM),
        scratch_shapes=[
            pltpu.VMEM((max(coeff_rows, tasks * width + spares), occupied), jnp.float32),
            pltpu.VMEM((2 * coeff_rows // width, width, occupied), jnp.bfloat16),
            pltpu.VMEM((2 * coeff_rows // width, width, occupied), jnp.bfloat16),
            pltpu.VMEM((2, coeff_rows // PIECES, occupied), jnp.float32),
            pltpu.VMEM((SLOTS, width, span), jnp.float32),
            pltpu.VMEM((tasks * width, occupied), jnp.float32),
            pltpu.VMEM((4 * half_rows, aux_local * occupied), jnp.bfloat16),
            pltpu.VMEM((far_count, slots) + square, jnp.float32),
            pltpu.VMEM((far_count + 1, slots) + square, jnp.float32),
            pltpu.VMEM((slots,) + square, jnp.float32),
            pltpu.VMEM((slots,) + square, jnp.float32),
            pltpu.SemaphoreType.DMA((2,)),
            pltpu.SemaphoreType.DMA((SLOTS,)),
            pltpu.SemaphoreType.DMA((2, PIECES)),
            pltpu.SemaphoreType.DMA((2, tasks)),
            pltpu.SemaphoreType.DMA((2, far_count, slots)),
            pltpu.SemaphoreType.DMA((2, far_count + 1, slots)),
            pltpu.SemaphoreType.DMA((2, slots)),
        ],
        compiler_params=pltpu.CompilerParams(
            collective_id=0, has_side_effects=True, vmem_limit_bytes=VMEM_LIMIT
        ),
        name="exchange",
    )(partner_blocks, block_counts, integrals, occupied_coeff)


def solution(mesh):
    placed = (
        P(("grp", "aux"), "bas", None, None),
        P(("grp", "aux"), "bas"),
        P(("grp", "aux"), "bas", None),
        P(("grp", "bas"), None),
    )
    return jax.shard_map(
        functools.partial(shards, mesh.shape["aux"]),
        mesh=mesh,
        in_specs=placed,
        out_specs=P(("grp", "aux"), "bas"),
        check_vma=False,
    )
```

time: 135 us -> 113 us (0.84)
  Pallas kernels: 131 us -> 110 us
    pallas_call x3 -> x1, Pallas kernels: 131 us -> 110 us  [shards(): pl.pallas_call(functools.partial(exchange_kernel, aux), out_shape=jax.Sha...]
where the time goes in v3:
time: 113 us
  Pallas kernels  110 us (97%)
  local copies, waits for them, and re-layouts  2.31 us (2%)
    pallas_call x1, Pallas kernels, shards(): pl.pallas_call(functools.partial(exchange_kernel, aux), out_shape=jax.Sha...  110 us
    unnamed x1, local copies, waits for them, and re-layouts  2.31 us

profile of v3, /device:TPU:1, one launch (start us, length us, event | category | flops | bytes accessed | tf_op | source)
XLA Modules:
  0.0 112.8 jit_solution(1347185083103148970)
XLA Ops:
  0.0 110.5 %exchange.1 = f32[256,1024]{1,0:T(8,128)} custom-call(s32[2,8,8]{2,1,0:T(8,128)} %lists_ref.1, s32[2,8]{1,0:T(2,128)} %counts_ref.1, f32[2,8,128,1024]{3,2,1,0:T(8,128)} %tiles_ref.1, f32[5120,512]{1,0:T(8,128)} %coeff_ref.1), custom_call_target="tpu_custom_call" | custom-call | tf_op jit(solution)/shard_map/exchange/pallas_call | solution.py:423
  110.5 2.3 %copy.6 = f32[256,1024]{1,0:T(8,128)} copy(f32[256,1024]{1,0:T(8,128)} %exchange.1) | data formatting | bytes 2097152

commit v4 on v3

--- a/solution.py
+++ b/solution.py
@@ -135,6 +135,9 @@
     def sum_at(target, k):
         return spare((far_count + target) * slots + k)
 
+    def square_at(target, k):
+        return near_at(target, keep) if k == slots else sum_at(target, k)
+
     def near_copy(step, k):
         return remote(
             land_ref.at[near_at(step, k)],
@@ -149,7 +152,7 @@
         last = down * (target == far - 1).astype(jnp.int32)
         place = target + last * (far_count - target)
         return pltpu.make_async_remote_copy(
-            src_ref=land_ref.at[sum_at(target, k)],
+            src_ref=land_ref.at[square_at(target, k)],
             dst_ref=far_recv.at[place, k],
             send_sem=far_sems.at[0, target, k],
             recv_sem=far_sems.at[1, place, k],
@@ -161,7 +164,7 @@
         pltpu.make_async_copy(
             far_recv.at[place, k], far_recv.at[place, k], far_sems.at[1, place, k]
         ).wait()
-        land_ref[sum_at(target, k)] += far_recv[place, k]
+        land_ref[square_at(target, k)] += far_recv[place, k]
 
     def target_at(step):
         upper = (far >= far_count // 2).astype(jnp.int32)
@@ -199,10 +202,20 @@
             },
         )
 
-    def blocks(far_index, work):
-        for k in range(keep):
-            work(k)
-        pl.when(in_half(far_index))(functools.partial(work, keep))
+    def between(target):
+        return jnp.logical_or(
+            jnp.logical_and(target > far, far > 0),
+            jnp.logical_and(target < far, far < far_count - 1),
+        )
+
+    def gather_far(k):
+        @pl.when(far > 0)
+        def _():
+            add_far(far, k, far)
+
+        @pl.when(far < far_count - 1)
+        def _():
+            add_far(far_count, k, far)
 
     def store_parts(values, half, task):
         row = half * (shell_local * width) + lax.rem(task, shell_local) * width
@@ -293,62 +306,81 @@
 
     def send_near(step, carry):
         target = target_at(step)
-        row = target * near_count + (1 - near)
-
-        def work(k):
-            land_ref[near_at(target, k)] = product(row, k)
+        for k in range(keep):
+            land_ref[near_at(target, k)] = product(target * near_count + (1 - near), k)
             near_copy(target, k).start()
-
-        blocks(target, work)
-        return carry
-
-    lax.fori_loop(0, far_count, send_near, 0)
+        return carry
+
+    lax.fori_loop(0, 1, send_near, 0)
+
+    def start_last(step, carry):
+        target = target_at(step)
+
+        @pl.when(in_half(target))
+        def _():
+            for k in (keep, slots):
+                index = near if k == keep else 1 - near
+                land_ref[square_at(target, k)] = product(target * near_count + index, keep)
+
+                @pl.when(jnp.logical_and(target != far, jnp.logical_not(between(target))))
+                def _():
+                    far_copy(target, k).start()
+
+        return carry
+
+    lax.fori_loop(0, far_count, start_last, 0)
+    lax.fori_loop(1, far_count, send_near, 0)
 
     def own_products(step, carry):
         target = target_at(step)
-
-        def work(k):
+        for k in range(keep):
             land_ref[sum_at(target, k)] = product(target * near_count + near, k)
-
-        blocks(target, work)
         return carry
 
     lax.fori_loop(0, far_count, own_products, 0)
+
+    def forward_last(step, carry):
+        target = target_at(step)
+
+        @pl.when(jnp.logical_and(in_half(target), between(target)))
+        def _():
+            for k in (keep, slots):
+                add_far(target, k, target)
+                far_copy(target, k).start()
+
+        return carry
+
+    lax.fori_loop(0, far_count - 1, forward_last, 0)
 
     def send_far(step, carry):
         target = target_at(step)
-        between = jnp.logical_or(
-            jnp.logical_and(target > far, far > 0),
-            jnp.logical_and(target < far, far < far_count - 1),
-        )
-
-        def work(k):
+        for k in range(keep):
             near_copy(target, k).wait_recv()
             land_ref[sum_at(target, k)] += near_recv[target, k]
 
-            @pl.when(between)
+            @pl.when(between(target))
             def _():
                 add_far(target, k, target)
 
             far_copy(target, k).start()
-
-        blocks(target, work)
-        return carry
-
-    lax.fori_loop(0, far_count - 1, send_far, 0)
+        return carry
+
+    lax.fori_loop(0, 1, send_far, 0)
+
+    @pl.when(in_half(far))
+    def _():
+        for k in (slots, keep):
+            gather_far(k)
+            if k == slots:
+                near_copy(far, keep).start()
+
+    lax.fori_loop(1, far_count - 1, send_far, 0)
 
     def finish(k):
         near_copy(far, k).wait_recv()
         land_ref[sum_at(far, k)] += near_recv[far, k]
-
-        @pl.when(far > 0)
-        def _():
-            add_far(far, k, far)
-
-        @pl.when(far < far_count - 1)
-        def _():
-            add_far(far_count, k, far)
-
+        if k < keep:
+            gather_far(k)
         total = land_ref[sum_at(far, k)]
         at = pl.multiple_of(column_of(position, k) * block, block)
         out_ref[:, pl.ds(at, block)] = total
@@ -396,15 +428,23 @@
     lax.fori_loop(0, tasks, half_done, 0)
 
     def near_done(step, carry):
-        target = target_at(step)
-        blocks(target, lambda k: near_copy(target, k).wait_send())
+        for k in range(keep):
+            near_copy(target_at(step), k).wait_send()
         return carry
 
     lax.fori_loop(0, far_count, near_done, 0)
+    pl.when(here)(lambda: near_copy(far, keep).wait_send())
 
     def far_done(step, carry):
         target = target_at(step)
-        blocks(target, lambda k: far_copy(target, k).wait_send())
+        for k in range(keep):
+            far_copy(target, k).wait_send()
+
+        @pl.when(in_half(target))
+        def _():
+            for k in (keep, slots):
+                far_copy(target, k).wait_send()
+
         return carry
 
     lax.fori_loop(0, far_count - 1, far_done, 0)
@@ -439,7 +479,7 @@
             pltpu.VMEM((tasks * width, occupied), jnp.float32),
             pltpu.VMEM((4 * half_rows, aux_local * occupied), jnp.bfloat16),
             pltpu.VMEM((far_count, slots) + square, jnp.float32),
-            pltpu.VMEM((far_count + 1, slots) + square, jnp.float32),
+            pltpu.VMEM((far_count + 1, slots + 1) + square, jnp.float32),
             pltpu.VMEM((slots,) + square, jnp.float32),
             pltpu.VMEM((slots,) + square, jnp.float32),
             pltpu.SemaphoreType.DMA((2,)),
@@ -447,7 +487,7 @@
             pltpu.SemaphoreType.DMA((2, PIECES)),
             pltpu.SemaphoreType.DMA((2, tasks)),
             pltpu.SemaphoreType.DMA((2, far_count, slots)),
-            pltpu.SemaphoreType.DMA((2, far_count + 1, slots)),
+            pltpu.SemaphoreType.DMA((2, far_count + 1, slots + 1)),
             pltpu.SemaphoreType.DMA((2, slots)),
         ],
         compiler_params=pltpu.CompilerParams(

time: 113 us -> 108 us (0.956)
  Pallas kernels: 110 us -> 105 us
    pallas_call x1, Pallas kernels: 110 us -> 105 us  [shards(): pl.pallas_call(functools.partial(exchange_kernel, aux), out_shape=jax.Sha...]
where the time goes in v4:
time: 108 us; the launch traced here: 107 us
  Pallas kernels  105 us (97%)
  local copies, waits for them, and re-layouts  2.31 us (2%)
    pallas_call x1, Pallas kernels, shards(): pl.pallas_call(functools.partial(exchange_kernel, aux), out_shape=jax.Sha...  105 us
    unnamed x1, local copies, waits for them, and re-layouts  2.31 us

profile of v4, /device:TPU:1, one launch (start us, length us, event | category | flops | bytes accessed | tf_op | source)
XLA Modules:
  0.0 107.3 jit_solution(4286720769898474941)
XLA Ops:
  0.0 105.0 %exchange.1 = f32[256,1024]{1,0:T(8,128)} custom-call(s32[2,8,8]{2,1,0:T(8,128)} %lists_ref.1, s32[2,8]{1,0:T(2,128)} %counts_ref.1, f32[2,8,128,1024]{3,2,1,0:T(8,128)} %tiles_ref.1, f32[5120,512]{1,0:T(8,128)} %coeff_ref.1), custom_call_target="tpu_custom_call" | custom-call | tf_op jit(solution)/shard_map/exchange/pallas_call | solution.py:463
  105.0 2.3 %copy.6 = f32[256,1024]{1,0:T(8,128)} copy(f32[256,1024]{1,0:T(8,128)} %exchange.1) | data formatting | bytes 2097152

commit v5 on v4

--- a/solution.py
+++ b/solution.py
@@ -63,8 +63,21 @@
     far = position // near_count
     near = lax.rem(position, near_count)
 
-    def tile_copy(task):
-        slot = lax.rem(task, SLOTS)
+    shells = block // width
+    group = shells * aux_local
+
+    def block_of(turn):
+        late = (turn >= keep).astype(jnp.int32)
+        return 2 * (turn - late * keep) + late * near + (1 - late) * (1 - near)
+
+    def task_of(order):
+        inner = lax.rem(order, group)
+        shell = block_of(order // group) * shells + lax.rem(inner, shells)
+        return (inner // shells) * shell_local + shell
+
+    def tile_copy(order):
+        slot = lax.rem(order, SLOTS)
+        task = task_of(order)
         return pltpu.make_async_copy(
             tiles_ref.at[task // shell_local, lax.rem(task, shell_local)],
             tile_ref.at[slot],
@@ -81,8 +94,8 @@
         )
 
     stage_copy(0).start()
-    for task in range(SLOTS):
-        tile_copy(task).start()
+    for order in range(SLOTS):
+        tile_copy(jnp.int32(order)).start()
 
     barrier = pltpu.get_barrier_semaphore()
     me = position * 2 + core
@@ -271,12 +284,13 @@
 
     lax.fori_loop(0, PIECES, split_landed, 0)
 
-    def one_task(task, carry):
-        tile_copy(task).wait()
+    def one_task(order, carry):
+        task = task_of(order)
+        tile_copy(order).wait()
         first, second = task // shell_local, lax.rem(task, shell_local)
         column = lax.broadcasted_iota(jnp.int32, (width, span), 1)
         tile = jnp.where(
-            column < counts_ref[first, second] * width, tile_ref[lax.rem(task, SLOTS)], 0.0
+            column < counts_ref[first, second] * width, tile_ref[lax.rem(order, SLOTS)], 0.0
         )
         blocks_here = [lists_ref[first, second, index] for index in range(listed)]
         row_high = jnp.concatenate([high_ref[block] for block in blocks_here], axis=0)
@@ -292,12 +306,25 @@
         land_ref[task_at(task), :] = half
         half_copy(task).start()
         store_parts(half, core, task)
-        pl.when(task + SLOTS < tasks)(lambda: tile_copy(task + SLOTS).start())
-        return carry
-
-    lax.fori_loop(0, tasks, one_task, 0)
-
-    def split_other(task, carry):
+        pl.when(order + SLOTS < tasks)(lambda: tile_copy(order + SLOTS).start())
+        return carry
+
+    def one_block(turn, carry):
+        lax.fori_loop(turn * group, (turn + 1) * group, one_task, 0)
+
+        @pl.when(turn < keep)
+        def _():
+            row = core * ring + block_of(turn)
+            target = row // near_count
+            land_ref[near_at(target, 0)] = product(row, 0)
+            near_copy(target, 0).start()
+
+        return carry
+
+    lax.fori_loop(0, ring, one_block, 0)
+
+    def split_other(order, carry):
+        task = task_of(order)
         half_copy(task).wait_recv()
         store_parts(other_ref[task_at(task), :], 1 - core, task)
         return carry
@@ -306,9 +333,14 @@
 
     def send_near(step, carry):
         target = target_at(step)
-        for k in range(keep):
+
+        def work(k):
             land_ref[near_at(target, k)] = product(target * near_count + (1 - near), k)
             near_copy(target, k).start()
+
+        pl.when(jnp.logical_not(in_half(target)))(functools.partial(work, 0))
+        for k in range(1, keep):
+            work(k)
         return carry
 
     lax.fori_loop(0, 1, send_near, 0)

time: 108 us -> 109 us (level)
  no operation moved by 1% of the time
where the time goes in v5:
time: 109 us; the launch traced here: 108 us
  Pallas kernels  106 us (97%)
  local copies, waits for them, and re-layouts  2.31 us (2%)
    pallas_call x1, Pallas kernels, shards(): pl.pallas_call(functools.partial(exchange_kernel, aux), out_shape=jax.Sha...  106 us
    unnamed x1, local copies, waits for them, and re-layouts  2.31 us

profile of v5, /device:TPU:1, one launch (start us, length us, event | category | flops | bytes accessed | tf_op | source)
XLA Modules:
  0.0 108.0 jit_solution(7867809077250238221)
XLA Ops:
  0.0 105.6 %exchange.1 = f32[256,1024]{1,0:T(8,128)} custom-call(s32[2,8,8]{2,1,0:T(8,128)} %lists_ref.1, s32[2,8]{1,0:T(2,128)} %counts_ref.1, f32[2,8,128,1024]{3,2,1,0:T(8,128)} %tiles_ref.1, f32[5120,512]{1,0:T(8,128)} %coeff_ref.1), custom_call_target="tpu_custom_call" | custom-call | tf_op jit(solution)/shard_map/exchange/pallas_call | solution.py:495
  105.7 2.3 %copy.6 = f32[256,1024]{1,0:T(8,128)} copy(f32[256,1024]{1,0:T(8,128)} %exchange.1) | data formatting | bytes 2097152

commit v6 on v5

--- a/solution.py
+++ b/solution.py
@@ -309,6 +309,24 @@
         pl.when(order + SLOTS < tasks)(lambda: tile_copy(order + SLOTS).start())
         return carry
 
+    def start_last(k):
+        index = near if k == keep else 1 - near
+
+        def start(step, carry):
+            target = target_at(step)
+
+            @pl.when(in_half(target))
+            def _():
+                land_ref[square_at(target, k)] = product(target * near_count + index, keep)
+
+                @pl.when(jnp.logical_and(target != far, jnp.logical_not(between(target))))
+                def _():
+                    far_copy(target, k).start()
+
+            return carry
+
+        lax.fori_loop(0, far_count, start, 0)
+
     def one_block(turn, carry):
         lax.fori_loop(turn * group, (turn + 1) * group, one_task, 0)
 
@@ -319,9 +337,11 @@
             land_ref[near_at(target, 0)] = product(row, 0)
             near_copy(target, 0).start()
 
+        pl.when(turn == keep - 1)(lambda: start_last(slots))
         return carry
 
     lax.fori_loop(0, ring, one_block, 0)
+    start_last(keep)
 
     def split_other(order, carry):
         task = task_of(order)
@@ -343,25 +363,20 @@
             work(k)
         return carry
 
-    lax.fori_loop(0, 1, send_near, 0)
-
-    def start_last(step, carry):
+    lax.fori_loop(0, far_count, send_near, 0)
+
+    def forward_last(step, carry):
         target = target_at(step)
 
-        @pl.when(in_half(target))
+        @pl.when(jnp.logical_and(in_half(target), between(target)))
         def _():
-            for k in (keep, slots):
-                index = near if k == keep else 1 - near
-                land_ref[square_at(target, k)] = product(target * near_count + index, keep)
-
-                @pl.when(jnp.logical_and(target != far, jnp.logical_not(between(target))))
-                def _():
-                    far_copy(target, k).start()
-
-        return carry
-
-    lax.fori_loop(0, far_count, start_last, 0)
-    lax.fori_loop(1, far_count, send_near, 0)
+            for k in (slots, keep):
+                add_far(target, k, target)
+                far_copy(target, k).start()
+
+        return carry
+
+    lax.fori_loop(0, far_count - 1, forward_last, 0)
 
     def own_products(step, carry):
         target = target_at(step)
@@ -370,19 +385,6 @@
         return carry
 
     lax.fori_loop(0, far_count, own_products, 0)
-
-    def forward_last(step, carry):
-        target = target_at(step)
-
-        @pl.when(jnp.logical_and(in_half(target), between(target)))
-        def _():
-            for k in (keep, slots):
-                add_far(target, k, target)
-                far_copy(target, k).start()
-
-        return carry
-
-    lax.fori_loop(0, far_count - 1, forward_last, 0)
 
     def send_far(step, carry):
         target = target_at(step)

time: 109 us -> 101 us (0.927)
  Pallas kernels: 106 us -> 97.9 us
    pallas_call x1, Pallas kernels: 106 us -> 97.9 us  [shards(): pl.pallas_call(functools.partial(exchange_kernel, aux), out_shape=jax.Sha...]
where the time goes in v6:
time: 101 us; the launch traced here: 100 us
  Pallas kernels  97.9 us (97%)
  local copies, waits for them, and re-layouts  2.31 us (2%)
    pallas_call x1, Pallas kernels, shards(): pl.pallas_call(functools.partial(exchange_kernel, aux), out_shape=jax.Sha...  97.9 us
    unnamed x1, local copies, waits for them, and re-layouts  2.31 us

profile of v6, /device:TPU:1, one launch (start us, length us, event | category | flops | bytes accessed | tf_op | source)
XLA Modules:
  0.0 100.2 jit_solution(18395145044846260130)
XLA Ops:
  0.0 97.9 %exchange.1 = f32[256,1024]{1,0:T(8,128)} custom-call(s32[2,8,8]{2,1,0:T(8,128)} %lists_ref.1, s32[2,8]{1,0:T(2,128)} %counts_ref.1, f32[2,8,128,1024]{3,2,1,0:T(8,128)} %tiles_ref.1, f32[5120,512]{1,0:T(8,128)} %coeff_ref.1), custom_call_target="tpu_custom_call" | custom-call | tf_op jit(solution)/shard_map/exchange/pallas_call | solution.py:497
  97.9 2.3 %copy.6 = f32[256,1024]{1,0:T(8,128)} copy(f32[256,1024]{1,0:T(8,128)} %exchange.1) | data formatting | bytes 2097152
